TPU v7x, 256 devices: a whole 4x4x8 slice. The times are simulated.
256 devices in a mesh: row: 32 (over x, z), col: 8 (over y, core).
Axes of the slice: x: 4, y: 4, z: 8, core: 2. Of those that a mesh axis runs over, the one named last changes fastest.
Arguments:
- features: bfloat16 [64, 32768], P(None, ('col', 'row')), may hold values from -4 to 4
- targets: float32 [128, 32768], P(None, ('col', 'row')), may hold values from -6 to 6
Outputs:
- coefficients: float32 [128, 32768], P(None, ('col', 'row'))
- residual: float32 [128, 32768], P(None, ('col', 'row'))
- direction: float32 [128, 32768], P(None, ('col', 'row'))
All inputs are finite; a program needn't handle non-finite values.
Results may differ from a plain program's by a relative error of at most 0.0061.
Values may be sent and summed in bfloat16 or wider, within the bound.
A program may use at most 64 MiB of HBM per device.

v0:
```python
import jax
import jax.numpy as jnp
from jax import lax
from jax.sharding import PartitionSpec as P

F = 64
ridge_weight = 0.5
kernel_gain = 2.0
sharpness = 3.0


def tile_term(rows_feat, rows_sq, cols_feat, cols_panel):
    cols_wide = cols_feat.astype(jnp.float32)
    cols_sq = jnp.sum(cols_wide * cols_wide, axis=0)
    total_rows = rows_feat.shape[1]
    block_size = min(512, total_rows)
    blocks = total_rows // block_size
    row_blocks = rows_feat.reshape(rows_feat.shape[0], blocks, block_size).transpose(1, 0, 2)
    sq_blocks = rows_sq.reshape(blocks, block_size)

    def block_image(operands):
        row_part, row_norms = operands
        inner = lax.dot_general(
            row_part, cols_feat, (((0,), (0,)), ((), ())), preferred_element_type=jnp.float32
        )
        distance = row_norms[:, None] + cols_sq[None, :] - 2.0 * inner
        entries = jnp.exp(-sharpness * distance / F).astype(jnp.bfloat16)
        return lax.dot_general(
            cols_panel, entries, (((1,), (1,)), ((), ())), preferred_element_type=jnp.float32
        )

    stacked = lax.map(block_image, (row_blocks, sq_blocks))
    return stacked.transpose(1, 0, 2).reshape(cols_panel.shape[0], total_rows)


def squared_norms(feat):
    wide = feat.astype(jnp.float32)
    return jnp.sum(wide * wide, axis=0)


def gram(left, right):
    return lax.dot_general(left, right, (((1,), (1,)), ((), ())), precision=lax.Precision.HIGHEST)


def cholesky_factor(matrix):
    size = matrix.shape[0]
    index = jnp.arange(size, dtype=jnp.int32)

    def step(position, state):
        rest, factor = state
        pos = jnp.asarray(position).astype(jnp.int32)
        column = lax.dynamic_slice_in_dim(rest, pos, 1, 1)[:, 0]
        pivot = jnp.sqrt(lax.dynamic_slice_in_dim(column, pos, 1, 0)[0])
        column = jnp.where(index >= pos, column / pivot, jnp.zeros_like(column))
        rest = rest - column[:, None] * column[None, :]
        factor = lax.dynamic_update_slice_in_dim(factor, column[:, None], pos, 1)
        return (rest, factor)

    return lax.fori_loop(0, size, step, (matrix, jnp.zeros_like(matrix)))[1]


def solve_with(factor, rhs):
    size = factor.shape[0]

    def forward(position, solved):
        pos = jnp.asarray(position).astype(jnp.int32)
        line = lax.dynamic_slice_in_dim(factor, pos, 1, 0)
        pivot = lax.dynamic_slice_in_dim(line[0], pos, 1, 0)[0]
        value = (
            lax.dynamic_slice_in_dim(rhs, pos, 1, 0)
            - jnp.dot(line, solved, precision=lax.Precision.HIGHEST)
        ) / pivot
        return lax.dynamic_update_slice_in_dim(solved, value, pos, 0)

    middle = lax.fori_loop(0, size, forward, jnp.zeros_like(rhs))

    def backward(step_count, solved):
        pos = (size - 1 - jnp.asarray(step_count)).astype(jnp.int32)
        line = lax.dynamic_slice_in_dim(factor, pos, 1, 1)
        pivot = lax.dynamic_slice_in_dim(line[:, 0], pos, 1, 0)[0]
        value = (
            lax.dynamic_slice_in_dim(middle, pos, 1, 0)
            - jnp.dot(line.T, solved, precision=lax.Precision.HIGHEST)
        ) / pivot
        return lax.dynamic_update_slice_in_dim(solved, value, pos, 0)

    return lax.fori_loop(0, size, backward, jnp.zeros_like(rhs))


def local(features, targets):
    panel = targets.astype(jnp.bfloat16)
    rows_feat = lax.all_gather(features, "col", axis=1, tiled=True)
    rows_sq = squared_norms(rows_feat)
    partial_image = tile_term(
        rows_feat,
        rows_sq,
        lax.all_gather(features, "row", axis=1, tiled=True),
        lax.all_gather(panel, "row", axis=1, tiled=True),
    )
    kernel_image = lax.psum_scatter(partial_image, "col", scatter_dimension=1, tiled=True)
    image = ridge_weight * targets + kernel_gain * kernel_image
    squares, curvature = lax.psum((gram(targets, targets), gram(targets, image)), ("row", "col"))
    sym = 0.5 * (curvature + curvature.T)
    factor = cholesky_factor(sym)
    step_size = solve_with(factor, squares)
    residual = targets - jnp.dot(step_size.T, image, precision=lax.Precision.HIGHEST)
    conjugacy = lax.psum(gram(image, residual), ("row", "col"))
    coefficients = jnp.dot(step_size.T, targets, precision=lax.Precision.HIGHEST)
    correction = -solve_with(factor, conjugacy)
    direction = residual + jnp.dot(correction.T, targets, precision=lax.Precision.HIGHEST)
    return (coefficients, residual, direction)


def solution(mesh):
    return jax.shard_map(
        local,
        mesh=mesh,
        in_specs=(P(None, ("col", "row")), P(None, ("col", "row"))),
        out_specs=(P(None, ("col", "row")), P(None, ("col", "row")), P(None, ("col", "row"))),
        check_vma=False,
    )
```

profile of v0, /device:TPU:1, one launch (start us, length us, event | category | flops | bytes accessed | tf_op | source)
XLA Modules:
  0.0 1720.8 jit_solution(16976305173994031126)
XLA Ops:
  8.8 14.6 all_gather.9
  23.5 41.9 %all_gather.10 = bf16[64,4096]{1,0:T(8,128)(2,1)S(1)} all-gather(bf16[64,128]{1,0:T(8,128)(2,1)} %param.14), channel_id=1, replica_groups=mesh['row'=32,'col'=8] {'row'}, dimensions={1}, use_global_device_ids=true | all-gather | bytes 540672 | tf_op jit(solution)/shard_map/all_gather | solution.py:97
  65.5 16.6 all-gather.2.cloned.1.call-done
  82.2 7.7 while.95
  82.2 3.8 fusion.65
  86.0 3.8 fusion.65
  91.7 33.0 %reduce-scatter.2.cloned.1.call-done = f32[128,128]{0,1:T(8,128)} async-done(((f32[128,1024]{0,1:T(8,128)}), f32[128,128]{0,1:T(8,128)}) %reduce-scatter.2.cloned.1.call-update) | async-done | bytes 65552 | tf_op jit(solution)/shard_map/reduce_scatter | solution.py:100
  124.7 1.8 convolution_bitcast_fusion
  126.6 247.5 %all-reduce.6.cloned.1.call-done = (f32[128,128]{1,0:T(8,128)}, f32[128,128]{0,1:T(8,128)}) async-done(((f32[128,128]{1,0:T(8,128)}, f32[128,128]{0,1:T(8,128)}), (f32[128,128]{1,0:T(8,128)}, f32[128,128]{0,1:T(8,128)})) %all-reduce.6.cloned.1.call-update) | async-done | bytes 131088 | tf_op jit(solution)/shard_map/psum | solution.py:102
  375.9 186.7 %while.100 = (s32[]{:T(128)}, f32[128,128]{0,1:T(8,128)S(1)}, f32[128,128]{0,1:T(8,128)S(1)}, s32[]{:T(128)}, s32[]{:T(128)}, /*index=5*/s32[]{:T(128)}) while((s32[]{:T(128)}, f32[128,128]{0,1:T(8,128)S(1)}, f32[128,128]{0,1:T(8,128)S(1)}, s32[]{:T(128)}, s32[]{:T(128)}, /*index=5*/s32[]{:T(128)}) %tuple.218), condition=%wide.region_7.8_spmd.clone, body=%wide.region_6.7_spmd.clone.sunk | while | flops 33411 | bytes 137329 | solution.py:59
  562.7 271.6 %while.96 = (s32[]{:T(128)}, f32[128,128]{1,0:T(8,128)S(1)}, f32[128,128]{1,0:T(8,128)}, f32[128,128]{1,0:T(8,128)S(1)}, s32[]{:T(128)}, /*index=5*/s32[]{:T(128)}, s32[]{:T(128)}) while((s32[]{:T(128)}, f32[128,128]{1,0:T(8,128)S(1)}, f32[128,128]{1,0:T(8,128)}, f32[128,128]{1,0:T(8,128)S(1)}, s32[]{:T(128)}, /*index=5*/s32[]{:T(128)}, ...), condition=%wide.region_10.11_spmd, body=%wide.region_9.10_spmd.sunk | while | flops 196867 | bytes 69741 | solution.py:75
  686.3 1.5 fusion.68
  688.4 1.5 fusion.68
  694.8 1.5 fusion.68
  696.9 1.5 fusion.68
  834.2 185.2 %while.97 = (s32[]{:T(128)}, f32[128,128]{1,0:T(8,128)S(1)}, f32[128,128]{1,0:T(8,128)S(1)}, f32[128,128]{0,1:T(8,128)S(1)}, s32[]{:T(128)}, /*index=5*/s32[]{:T(128)}, s32[]{:T(128)}, s32[]{:T(128)}) while((s32[]{:T(128)}, f32[128,128]{1,0:T(8,128)S(1)}, f32[128,128]{1,0:T(8,128)S(1)}, f32[128,128]{0,1:T(8,128)S(1)}, s32[]{:T(128)}, ...), condition=%wide.region_12.13_spmd, body=%wide.region_11.12_spmd.sunk | while | flops 196871 | bytes 69287 | solution.py:87
  1021.6 234.9 %all-reduce.4.cloned.1.call-done = f32[128,128]{1,0:T(8,128)} async-done(((f32[128,128]{1,0:T(8,128)}), f32[128,128]{1,0:T(8,128)}) %all-reduce.4.cloned.1.call-update) | async-done | bytes 65552 | tf_op jit(solution)/shard_map/psum | solution.py:107
  1256.5 271.6 %while.98 = (s32[]{:T(128)}, f32[128,128]{1,0:T(8,128)S(1)}, f32[128,128]{1,0:T(8,128)}, f32[128,128]{1,0:T(8,128)S(1)}, s32[]{:T(128)}, /*index=5*/s32[]{:T(128)}, s32[]{:T(128)}) while((s32[]{:T(128)}, f32[128,128]{1,0:T(8,128)S(1)}, f32[128,128]{1,0:T(8,128)}, f32[128,128]{1,0:T(8,128)S(1)}, s32[]{:T(128)}, /*index=5*/s32[]{:T(128)}, ...), condition=%wide.region_15.16_spmd, body=%wide.region_14.15_spmd.sunk | while | flops 196867 | bytes 69741 | solution.py:75
  1376.0 1.5 fusion.74
  1378.1 1.5 fusion.74
  1380.2 1.5 fusion.74
  1382.3 1.5 fusion.74
  1384.5 1.5 fusion.74
  1528.2 185.2 %while.99 = (s32[]{:T(128)}, f32[128,128]{1,0:T(8,128)S(1)}, f32[128,128]{1,0:T(8,128)S(1)}, f32[128,128]{0,1:T(8,128)S(1)}, s32[]{:T(128)}, /*index=5*/s32[]{:T(128)}, s32[]{:T(128)}, s32[]{:T(128)}) while((s32[]{:T(128)}, f32[128,128]{1,0:T(8,128)S(1)}, f32[128,128]{1,0:T(8,128)S(1)}, f32[128,128]{0,1:T(8,128)S(1)}, s32[]{:T(128)}, ...), condition=%wide.region_17.18_spmd, body=%wide.region_16.17_spmd.sunk | while | flops 196871 | bytes 69287 | solution.py:87
  (2206 shorter events, 987.9 us)
Async XLA Ops:
  7.2 75.0 %all-gather.2.cloned.1.call-start = ((), (), s32[]{:S(2)}) async-start(), calls=%async_computation.1 | async-start | bytes 1081344 | tf_op jit(solution)/shard_map/all_gather | solution.py:98
  8.7 116.0 %reduce-scatter.2.cloned.1.call-start = ((), (), s32[]{:S(2)}) async-start(), calls=%async_computation.2 | async-start | bytes 589824 | tf_op jit(solution)/shard_map/reduce_scatter | solution.py:100
  82.2 8.5 copy-start
  89.8 0.8 copy-start.3
  90.6 283.4 %all-reduce.6.cloned.1.call-start = ((), (), s32[]{:S(2)}) async-start(), calls=%async_computation.4 | async-start | bytes 262144 | tf_op jit(solution)/shard_map/psum | solution.py:102
  126.5 1130.0 %all-reduce.4.cloned.1.call-start = ((), (), s32[]{:S(2)}) async-start(), calls=%async_computation.3 | async-start | bytes 131072 | tf_op jit(solution)/shard_map/psum | solution.py:107
  375.8 643.6 %copy-start.1 = (f32[128,128]{0,1:T(8,128)S(1)}, f32[128,128]{0,1:T(8,128)}, u32[]{:S(2)}) copy-start(f32[128,128]{0,1:T(8,128)} %reduce-scatter.2.cloned.1.call-done) | copy-start | bytes 196612
  1019.7 694.6 %copy-start.2 = (f32[128,128]{1,0:T(8,128)}, f32[128,128]{1,0:T(8,128)S(1)}, u32[]{:S(2)}) copy-start(f32[128,128]{1,0:T(8,128)S(1)} %convolution_subtract_fusion.4) | copy-start | bytes 196612
Sparse Core Ops, SparseCore 0:
  11.0 71.0 all-gather.1
  90.8 33.9 reduce-scatter.1
  131.8 242.1 all-reduce.5
  1020.8 235.6 all-reduce.3
where the time goes:
time: 1740 us; the launch traced here: 1720 us
  matrix products  596 us (34%)
  waiting for transfers between devices  532 us (31%)
  local copies, waits for them, and re-layouts  399 us (23%)
  loops' own time  108 us (6%)
  blocking collectives  56.5 us (3%)
    dot_general x256, matrix products, forward(): jnp.dot(line, solved, precision=lax.Precision.HIGHEST)  379 us
    psum x1, waiting for transfers between devices, local(): lax.psum((gram(targets, targets), gram(targets, image)), ('row', 'col'))  247 us
    psum x1, waiting for transfers between devices, local(): conjugacy = lax.psum(gram(image, residual), ('row', 'col'))  235 us
    dot_general x256, matrix products, backward(): jnp.dot(line.T, solved, precision=lax.Precision.HIGHEST)  204 us
    dynamic_slice x256, local copies, waits for them, and re-layouts, backward(): pivot = lax.dynamic_slice_in_dim(line[:, 0], pos, 1, 0)[0]  151 us
    dynamic_slice x256, local copies, waits for them, and re-layouts, forward(): pivot = lax.dynamic_slice_in_dim(line[0], pos, 1, 0)[0]  151 us
    another operation x1, loops' own time, cholesky_factor(): return lax.fori_loop(0, size, step, (matrix, jnp.zeros_like(matrix)))[1]  93.8 us
    dynamic_slice x128, local copies, waits for them, and re-layouts, step(): pivot = jnp.sqrt(lax.dynamic_slice_in_dim(column, pos, 1, 0)[0])  75.3 us
  transfers between devices with their start and end apart: 4, of which 4 were waited for; matrix products, arithmetic and copies ran while one was open for 0% of the time, Pallas kernels for 0%

commit v1 on v0

--- a/solution.py
+++ b/solution.py
@@ -104,7 +104,7 @@
     factor = cholesky_factor(sym)
     step_size = solve_with(factor, squares)
     residual = targets - jnp.dot(step_size.T, image, precision=lax.Precision.HIGHEST)
-    conjugacy = lax.psum(gram(image, residual), ("row", "col"))
+    conjugacy = jnp.sum(lax.all_gather(gram(image, residual), ("row", "col")), axis=0)
     coefficients = jnp.dot(step_size.T, targets, precision=lax.Precision.HIGHEST)
     correction = -solve_with(factor, conjugacy)
     direction = residual + jnp.dot(correction.T, targets, precision=lax.Precision.HIGHEST)

time: 1740 us -> 1540 us (0.89)
  waiting for transfers between devices: 532 us -> 419 us
  matrix products: 596 us -> 510 us
    psum x1 -> x0, waiting for transfers between devices: 235 us -> none  [local(): conjugacy = lax.psum(gram(image, residual), ('row', 'col'))]
    all_gather x0 -> x1, waiting for transfers between devices: none -> 122 us  [local(): lax.all_gather(gram(image, residual), ('row', 'col'))]
    dot_general x256, matrix products: 379 us -> 291 us  [forward(): jnp.dot(line, solved, precision=lax.Precision.HIGHEST)]
where the time goes in v1:
time: 1540 us; the launch traced here: 1530 us
  matrix products  510 us (33%)
  waiting for transfers between devices  419 us (27%)
  local copies, waits for them, and re-layouts  399 us (26%)
  loops' own time  108 us (7%)
  blocking collectives  56.5 us (4%)
  other arithmetic  21.9 us (1%)
    dot_general x256, matrix products, forward(): jnp.dot(line, solved, precision=lax.Precision.HIGHEST)  291 us
    psum x1, waiting for transfers between devices, local(): lax.psum((gram(targets, targets), gram(targets, image)), ('row', 'col'))  247 us
    dot_general x256, matrix products, backward(): jnp.dot(line.T, solved, precision=lax.Precision.HIGHEST)  204 us
    dynamic_slice x256, local copies, waits for them, and re-layouts, backward(): pivot = lax.dynamic_slice_in_dim(line[:, 0], pos, 1, 0)[0]  151 us
    dynamic_slice x256, local copies, waits for them, and re-layouts, forward(): pivot = lax.dynamic_slice_in_dim(line[0], pos, 1, 0)[0]  151 us
    all_gather x1, waiting for transfers between devices, local(): lax.all_gather(gram(image, residual), ('row', 'col'))  122 us
    another operation x1, loops' own time, cholesky_factor(): return lax.fori_loop(0, size, step, (matrix, jnp.zeros_like(matrix)))[1]  93.8 us
    dynamic_slice x128, local copies, waits for them, and re-layouts, step(): pivot = jnp.sqrt(lax.dynamic_slice_in_dim(column, pos, 1, 0)[0])  75.3 us
  transfers between devices with their start and end apart: 4, of which 4 were waited for; matrix products, arithmetic and copies ran while one was open for 0% of the time, Pallas kernels for 0%

profile of v1, /device:TPU:1, one launch (start us, length us, event | category | flops | bytes accessed | tf_op | source)
XLA Modules:
  0.0 1529.2 jit_solution(8453066575609377514)
XLA Ops:
  8.8 14.6 all_gather.15
  23.5 41.9 %all_gather.16 = bf16[64,4096]{1,0:T(8,128)(2,1)S(1)} all-gather(bf16[64,128]{1,0:T(8,128)(2,1)} %param.14), channel_id=1, replica_groups=mesh['row'=32,'col'=8] {'row'}, dimensions={1}, use_global_device_ids=true | all-gather | bytes 540672 | tf_op jit(solution)/shard_map/all_gather | solution.py:97
  65.5 16.6 %all-gather.4.cloned.1.call-done = bf16[128,4096]{1,0:T(8,128)(2,1)} async-done(((bf16[128,128]{1,0:T(8,128)(2,1)}), bf16[128,4096]{1,0:T(8,128)(2,1)}) %all-gather.4.cloned.1.call-update) | async-done | bytes 1048592 | tf_op jit(solution)/shard_map/all_gather | solution.py:98
  82.2 7.7 while.95
  82.2 3.8 fusion.65
  86.0 3.8 fusion.65
  91.7 33.0 %reduce-scatter.2.cloned.1.call-done = f32[128,128]{0,1:T(8,128)} async-done(((f32[128,1024]{0,1:T(8,128)}), f32[128,128]{0,1:T(8,128)}) %reduce-scatter.2.cloned.1.call-update) | async-done | bytes 65552 | tf_op jit(solution)/shard_map/reduce_scatter | solution.py:100
  124.7 1.8 convolution_bitcast_fusion
  126.6 247.5 %all-reduce.3.cloned.1.call-done = (f32[128,128]{1,0:T(8,128)}, f32[128,128]{0,1:T(8,128)}) async-done(((f32[128,128]{1,0:T(8,128)}, f32[128,128]{0,1:T(8,128)}), (f32[128,128]{1,0:T(8,128)}, f32[128,128]{0,1:T(8,128)})) %all-reduce.3.cloned.1.call-update) | async-done | bytes 131088 | tf_op jit(solution)/shard_map/psum | solution.py:102
  375.9 186.7 %while.100 = (s32[]{:T(128)}, f32[128,128]{0,1:T(8,128)S(1)}, f32[128,128]{0,1:T(8,128)S(1)}, s32[]{:T(128)}, s32[]{:T(128)}, /*index=5*/s32[]{:T(128)}) while((s32[]{:T(128)}, f32[128,128]{0,1:T(8,128)S(1)}, f32[128,128]{0,1:T(8,128)S(1)}, s32[]{:T(128)}, s32[]{:T(128)}, /*index=5*/s32[]{:T(128)}) %tuple.218), condition=%wide.region_7.8_spmd.clone, body=%wide.region_6.7_spmd.clone.sunk | while | flops 33411 | bytes 137329 | solution.py:59
  562.7 271.5 %while.96 = (s32[]{:T(128)}, f32[128,128]{1,0:T(8,128)S(1)}, f32[128,128]{1,0:T(8,128)}, f32[128,128]{1,0:T(8,128)S(1)}, s32[]{:T(128)}, /*index=5*/s32[]{:T(128)}, s32[]{:T(128)}) while((s32[]{:T(128)}, f32[128,128]{1,0:T(8,128)S(1)}, f32[128,128]{1,0:T(8,128)}, f32[128,128]{1,0:T(8,128)S(1)}, s32[]{:T(128)}, /*index=5*/s32[]{:T(128)}, ...), condition=%wide.region_10.11_spmd, body=%wide.region_9.10_spmd.sunk | while | flops 196867 | bytes 69741 | solution.py:75
  749.9 1.5 fusion.68
  752.1 1.5 fusion.68
  754.2 1.5 fusion.68
  756.3 1.5 fusion.68
  758.5 1.5 fusion.68
  762.7 1.5 fusion.68
  764.8 1.5 fusion.68
  834.2 185.2 %while.97 = (s32[]{:T(128)}, f32[128,128]{1,0:T(8,128)S(1)}, f32[128,128]{1,0:T(8,128)S(1)}, f32[128,128]{0,1:T(8,128)S(1)}, s32[]{:T(128)}, /*index=5*/s32[]{:T(128)}, s32[]{:T(128)}, s32[]{:T(128)}) while((s32[]{:T(128)}, f32[128,128]{1,0:T(8,128)S(1)}, f32[128,128]{1,0:T(8,128)S(1)}, f32[128,128]{0,1:T(8,128)S(1)}, s32[]{:T(128)}, ...), condition=%wide.region_12.13_spmd, body=%wide.region_11.12_spmd.sunk | while | flops 196871 | bytes 69287 | solution.py:87
  1020.5 1.8 fusion.29
  1023.3 122.3 %all-gather.6.cloned.1.call-done = f32[32768,128]{1,0:T(8,128)} async-done(((f32[128,128]{1,0:T(8,128)}), f32[32768,128]{1,0:T(8,128)}) %all-gather.6.cloned.1.call-update) | async-done | bytes 16777232 | tf_op jit(solution)/shard_map/all_gather | solution.py:107
  1145.6 6.6 reduce_sum.29
  1152.2 184.3 %while.98 = (s32[]{:T(128)}, f32[128,128]{1,0:T(8,128)S(1)}, f32[128,128]{1,0:T(8,128)S(1)}, f32[128,128]{1,0:T(8,128)S(1)}, s32[]{:T(128)}, /*index=5*/s32[]{:T(128)}, s32[]{:T(128)}) while((s32[]{:T(128)}, f32[128,128]{1,0:T(8,128)S(1)}, f32[128,128]{1,0:T(8,128)S(1)}, f32[128,128]{1,0:T(8,128)S(1)}, s32[]{:T(128)}, ...), condition=%wide.region_15.16_spmd, body=%wide.region_14.15_spmd.sunk | while | flops 196867 | bytes 69741 | solution.py:75
  1336.5 185.2 %while.99 = (s32[]{:T(128)}, f32[128,128]{1,0:T(8,128)S(1)}, f32[128,128]{1,0:T(8,128)S(1)}, f32[128,128]{0,1:T(8,128)S(1)}, s32[]{:T(128)}, /*index=5*/s32[]{:T(128)}, s32[]{:T(128)}, s32[]{:T(128)}) while((s32[]{:T(128)}, f32[128,128]{1,0:T(8,128)S(1)}, f32[128,128]{1,0:T(8,128)S(1)}, f32[128,128]{0,1:T(8,128)S(1)}, s32[]{:T(128)}, ...), condition=%wide.region_17.18_spmd, body=%wide.region_16.17_spmd.sunk | while | flops 196871 | bytes 69287 | solution.py:87
  (2205 shorter events, 903.5 us)
Async XLA Ops:
  7.2 75.0 %all-gather.4.cloned.1.call-start = ((), (), s32[]{:S(2)}) async-start(), calls=%async_computation.1 | async-start | bytes 1081344 | tf_op jit(solution)/shard_map/all_gather | solution.py:98
  8.7 116.0 %reduce-scatter.2.cloned.1.call-start = ((), (), s32[]{:S(2)}) async-start(), calls=%async_computation.2 | async-start | bytes 589824 | tf_op jit(solution)/shard_map/reduce_scatter | solution.py:100
  82.2 8.5 copy-start
  89.8 0.8 copy-start.2
  90.6 283.4 %all-reduce.3.cloned.1.call-start = ((), (), s32[]{:S(2)}) async-start(), calls=%async_computation.4 | async-start | bytes 262144 | tf_op jit(solution)/shard_map/psum | solution.py:102
  126.5 1019.0 %all-gather.6.cloned.1.call-start = ((), (), s32[]{:S(2)}) async-start(), calls=%async_computation.3 | async-start | bytes 16842752 | tf_op jit(solution)/shard_map/all_gather | solution.py:107
  1020.5 501.2 %copy-start.1 = (f32[128,128]{1,0:T(8,128)}, f32[128,128]{1,0:T(8,128)S(1)}, u32[]{:S(2)}) copy-start(f32[128,128]{1,0:T(8,128)S(1)} %convolution_subtract_fusion.4) | copy-start | bytes 196612
Sparse Core Ops, SparseCore 0:
  11.0 71.0 all-gather.3
  90.8 33.9 reduce-scatter.1
  131.8 242.1 all-reduce.2
  1022.5 123.0 all-gather.5
